TPU v7x, 512 devices: a whole 4x4x16 slice. The times are simulated.
512 devices in a mesh: aux: 32 (over x_hi, z), occ: 4 (over y), vir: 4 (over x_lo, core).
Axes of the slice: x: 4 (x_hi: 2, x_lo: 2; x = x_hi * 2 + x_lo), y: 4, z: 16, core: 2. Of those that a mesh axis runs over, the one named last changes fastest.
Arguments:
- start_block: float32 [8, 80, 512], P(None, 'occ', 'vir'), may hold values from -6 to 6
- factors: bfloat16 [2, 8192, 80, 512], P(None, 'aux', 'occ', 'vir'), may hold values from -0.0625 to 0.0625
- eps_occ: float32 [80], P('occ'), may hold values from -1.2 to -0.3
- eps_vir: float32 [512], P('vir'), may hold values from 0.1 to 1.5
Outputs:
- coefficients: float32 [4, 8, 8], replicated
- next_block: float32 [8, 80, 512], P(None, 'occ', 'vir')
All inputs are finite; a program needn't handle non-finite values.
Results may differ from a plain program's by a relative error of at most 0.007.
Values sent between devices are 32-bit elements; how exact they have to be, the bound alone decides.
A program may use at most 64 MiB of HBM per device.

v0:
```python
import jax
import jax.numpy as jnp
from jax import lax
from jax.experimental import pallas as pl
from jax.experimental.pallas import tpu as pltpu
from jax.sharding import PartitionSpec as P

AUX_WAYS, OCC_WAYS, VIR_WAYS = 32, 4, 4
NV, ROWS, LANES, DEPTH = 8, 20, 128, 256
PAIRS = 40960
TILES = ROWS + 1
STRIDE, UNSTRIDE = 3, 11
GROUP = 4
MESH = pl.DeviceIdType.MESH
f32, bf16 = jnp.float32, jnp.bfloat16


def split(value):
    high = value.astype(bf16)
    low = (value - high.astype(f32)).astype(bf16)
    return jnp.concatenate([high, low], axis=0)


def merge(value):
    return value[:NV] + value[NV:]


def apply(matrix, value, first=0):
    total = matrix[:, first:first + 1] * value[0:1, :]
    for m in range(1, NV):
        total = total + matrix[:, first + m:first + m + 1] * value[m:m + 1, :]
    return total


def iotas():
    return (
        lax.broadcasted_iota(jnp.int32, (NV, LANES), 0),
        lax.broadcasted_iota(jnp.int32, (NV, LANES), 1),
    )


def factor(gram):
    row, lane = iotas()
    work = jnp.where(lane < NV, gram, jnp.where(lane == row + NV, 1.0, 0.0))
    scale = jnp.ones((NV, 1), f32)
    rows1 = lax.broadcasted_iota(jnp.int32, (NV, 1), 0)
    for k in range(NV):
        pivot = work[k:k + 1, k:k + 1]
        scale = jnp.where(rows1 == k, pivot, scale)
        if k < NV - 1:
            ratio = jnp.where(rows1 > k, work[:, k:k + 1] / pivot, 0.0)
            work = work - ratio * work[k:k + 1, :]
    return work * (1.0 / jnp.sqrt(scale))


def columns(sums):
    _, lane = iotas()
    out = jnp.zeros((NV, LANES), f32)
    for m, value in enumerate(sums):
        out = jnp.where(lane == m, jnp.sum(value, axis=1, keepdims=True), out)
    return out


def products(lefts, rights):
    sums = []
    for m in range(NV):
        total = lefts[0] * rights[0][m:m + 1, :]
        for left, right in zip(lefts[1:], rights[1:]):
            total = total + left * right[m:m + 1, :]
        sums.append(total)
    return sums


def kernel(
    start_hbm, fac_hbm, occ_hbm, vir_hbm,
    coef_ref, resid_ref,
    start, fac, eocc, evir, q1, q2, r1, xhat,
    cvir, cocc, part, rs, ag, mine, gm,
    in_sem, fac_sem, cv_send, cv_recv, co_send, co_recv,
    rs_send, rs_recv, ag_send, ag_recv, g_send, g_recv,
):
    aux = lax.axis_index("aux")
    occ = lax.axis_index("occ")
    vir = lax.axis_index("vir")
    spot = occ * VIR_WAYS + vir
    core = lax.rem(vir, 2)

    def tile_of(device):
        return lax.rem((device + core) * UNSTRIDE, AUX_WAYS)

    tile = tile_of(aux)
    owner = tile < TILES

    loads = [
        pltpu.make_async_copy(start_hbm, start, in_sem.at[0]),
        pltpu.make_async_copy(occ_hbm, eocc, in_sem.at[1]),
        pltpu.make_async_copy(vir_hbm, evir, in_sem.at[2]),
    ]
    fac_loads = [
        pltpu.make_async_copy(
            fac_hbm.at[:, pl.ds(GROUP * c, GROUP)], fac.at[:, pl.ds(GROUP * c, GROUP)], fac_sem.at[c]
        )
        for c in range(ROWS // GROUP)
    ]
    for load in loads + fac_loads:
        load.start()

    barrier = pltpu.get_barrier_semaphore()

    def greet_aux(d, carry):
        pl.semaphore_signal(
            barrier, inc=1, device_id={"aux": lax.rem(aux + d, AUX_WAYS)}, device_id_type=MESH
        )
        return carry

    def greet_spot(d, carry):
        other = lax.rem(spot + d, OCC_WAYS * VIR_WAYS)
        pl.semaphore_signal(
            barrier, inc=1,
            device_id={"occ": other // VIR_WAYS, "vir": lax.rem(other, VIR_WAYS)}, device_id_type=MESH,
        )
        return carry

    lax.fori_loop(1, AUX_WAYS, greet_aux, 0)
    lax.fori_loop(1, OCC_WAYS * VIR_WAYS, greet_spot, 0)

    for load in loads:
        load.wait()

    def delta(i):
        return evir[...] - eocc[i]

    def contract(source, waits):
        sums = [None, None]
        for i in range(0, ROWS, 2):
            if waits and i % GROUP == 0:
                fac_loads[i // GROUP].wait()
            left = jnp.concatenate([split(source[i]), split(source[i + 1])], axis=1)
            for s in range(2):
                right = jnp.concatenate([fac[s, i], fac[s, i + 1]], axis=1)
                term = lax.dot_general(
                    left, right, (((1,), (1,)), ((), ())), preferred_element_type=f32
                )
                sums[s] = term if sums[s] is None else sums[s] + term
        return [merge(sums[s])[:, LANES * h:LANES * (h + 1)] for s in range(2) for h in range(2)]

    def wait_bytes(ref, sem):
        pltpu.make_async_copy(ref, ref, sem).wait()

    def sum_group(step, tiles, first):
        count = len(tiles)
        for index, value in enumerate(tiles):
            cvir[step, vir, index] = value
        if first:
            pl.semaphore_wait(barrier, AUX_WAYS - 1 + OCC_WAYS * VIR_WAYS - 1)
        for d in range(1, VIR_WAYS):
            pltpu.make_async_remote_copy(
                src_ref=cvir.at[step, vir], dst_ref=cvir.at[step, vir],
                send_sem=cv_send.at[step], recv_sem=cv_recv.at[step],
                device_id={"vir": lax.rem(vir + d, VIR_WAYS)}, device_id_type=MESH,
            ).start()
        wait_bytes(cvir.at[step, pl.ds(0, VIR_WAYS - 1)], cv_recv.at[step])
        for index in range(count):
            cocc[step, occ, index] = (
                (cvir[step, 0, index] + cvir[step, 1, index])
                + (cvir[step, 2, index] + cvir[step, 3, index])
            )
        for d in range(1, OCC_WAYS):
            pltpu.make_async_remote_copy(
                src_ref=cocc.at[step, occ], dst_ref=cocc.at[step, occ],
                send_sem=co_send.at[step], recv_sem=co_recv.at[step],
                device_id={"occ": lax.rem(occ + d, OCC_WAYS)}, device_id_type=MESH,
            ).start()
        wait_bytes(cocc.at[step, pl.ds(0, OCC_WAYS - 1)], co_recv.at[step])
        return [
            (cocc[step, 0, index] + cocc[step, 1, index])
            + (cocc[step, 2, index] + cocc[step, 3, index])
            for index in range(count)
        ]

    def both_ways(action):
        def body(d, carry):
            action(d)
            action(AUX_WAYS - d)
            return carry

        lax.fori_loop(1, AUX_WAYS // 2, body, 0)
        action(AUX_WAYS // 2)

    def send_tile(step, t, target):
        pltpu.make_async_remote_copy(
            src_ref=part.at[step, t], dst_ref=rs.at[step, aux],
            send_sem=rs_send.at[step], recv_sem=rs_recv.at[step],
            device_id={"aux": target}, device_id_type=MESH,
        ).start()

    def send_rows(step):
        def action(d):
            target = lax.rem(aux + d, AUX_WAYS)
            t = tile_of(target)

            @pl.when(t < ROWS)
            def _():
                send_tile(step, t, target)

        both_ways(action)

        @pl.when(tile < ROWS)
        def _():
            rs[step, aux] = part[step, tile]

    def send_small(step):
        target = lax.rem(ROWS * STRIDE - core, AUX_WAYS)

        @pl.when(target != aux)
        def _():
            send_tile(step, ROWS, target)

        @pl.when(target == aux)
        def _():
            rs[step, aux] = part[step, ROWS]

    def back(step, sums):
        scaled = [
            split(jnp.concatenate([2.0 * sums[0], 2.0 * sums[1]], axis=1)),
            split(jnp.concatenate([-sums[2], -sums[3]], axis=1)),
        ]
        for i in range(0, ROWS, 2):
            both = None
            for s in range(2):
                right = jnp.concatenate([fac[s, i], fac[s, i + 1]], axis=1)
                term = lax.dot_general(
                    scaled[s], right, (((1,), (0,)), ((), ())), preferred_element_type=f32
                )
                both = term if both is None else both + term
            both = merge(both)
            part[step, i] = both[:, :LANES]
            part[step, i + 1] = both[:, LANES:]
        send_rows(step)

    def spread(step, lower, extra):
        @pl.when(owner)
        def _():
            wait_bytes(rs.at[step, pl.ds(0, AUX_WAYS - 1)], rs_recv.at[step])
            sums = [rs[step, j] for j in range(AUX_WAYS)]
            while len(sums) > 1:
                sums = [a + b for a, b in zip(sums[0::2], sums[1::2])]

            @pl.when(tile < ROWS)
            def _():
                mine[step] = apply(lower, sums[0], NV)

            @pl.when(tile == ROWS)
            def _():
                mine[step] = (sums[0] + extra) * (1.0 / PAIRS)

            def action(d):
                pltpu.make_async_remote_copy(
                    src_ref=mine.at[step], dst_ref=ag.at[step, tile],
                    send_sem=ag_send.at[step], recv_sem=ag_recv.at[step],
                    device_id={"aux": lax.rem(aux + d, AUX_WAYS)}, device_id_type=MESH,
                ).start()

            both_ways(action)
            ag[step, tile] = mine[step]
            wait_bytes(ag.at[step, pl.ds(0, TILES - 1)], ag_recv.at[step])

        @pl.when(jnp.logical_not(owner))
        def _():
            wait_bytes(ag.at[step], ag_recv.at[step])

    def small(left, right):
        return lax.dot_general(
            left, right, (((1,), (1,)), ((), ())),
            precision=lax.Precision.HIGHEST, preferred_element_type=f32,
        )

    def wide(value):
        return jnp.concatenate(
            [value, jnp.zeros((value.shape[0], LANES - value.shape[1]), f32)], axis=1
        )

    row, lane = iotas()
    weights = [2.0, 2.0, -1.0, -1.0]

    vecs = [start[i] for i in range(ROWS)]
    shifted = [vecs[i] * delta(i) for i in range(ROWS)]
    grams = columns(products(vecs, vecs) + products(vecs, shifted))
    sums = contract(vecs, True)
    *sums, grams = sum_group(0, sums + [grams], True)
    back(0, sums)
    lower = factor(grams * (1.0 / PAIRS))
    inverse = lower[:, NV:2 * NV]
    hats = [apply(lower, value, NV) for value in sums]
    for index in range(4):
        xhat[index] = hats[index]
    part[0, ROWS] = columns(products([w * hat for w, hat in zip(weights, hats)], hats))
    send_small(0)
    middle = small(small(inverse, grams[:, NV:2 * NV]), inverse)
    for i in range(ROWS):
        q1[i] = apply(lower, start[i], NV)
    spread(0, lower, wide(middle))
    proj = ag[0, ROWS]
    coef_ref[0] = proj
    for i in range(ROWS):
        r1[i] = ag[0, i] + delta(i) * q1[i] - apply(proj, q1[i])

    vecs = [r1[i] for i in range(ROWS)]
    moved = [delta(i) * q1[i] for i in range(ROWS)]
    shifted = [vecs[i] * delta(i) for i in range(ROWS)]
    grams = columns(products(vecs, vecs) + products(vecs, shifted) + products(vecs, moved))
    sums = contract(vecs, False)
    *sums, grams = sum_group(1, sums + [grams], False)
    back(1, sums)
    lower = factor(grams * (1.0 / PAIRS))
    inverse = lower[:, NV:2 * NV]
    hats = [apply(lower, value, NV) for value in sums]
    scaled = [w * hat for w, hat in zip(weights, hats)]
    part[1, ROWS] = columns(products(scaled, hats) + products(scaled, [xhat[k] for k in range(4)]))
    send_small(1)
    middle = small(small(inverse, grams[:, NV:2 * NV]), inverse)
    across = apply(lower, grams[:, 2 * NV:3 * NV], NV)
    coef_ref[1] = jnp.where(lane >= row, lower, 0.0)
    for i in range(ROWS):
        q2[i] = apply(lower, r1[i], NV)
    spread(1, lower, wide(jnp.concatenate([middle, across], axis=1)))
    proj = ag[1, ROWS]
    coef_ref[2] = proj
    for i in range(ROWS):
        resid_ref[i] = ag[1, i] + delta(i) * q2[i] - apply(proj, q2[i]) - apply(proj, q1[i], NV)

    vecs = [resid_ref[i] for i in range(ROWS)]
    gm[spot] = columns(products(vecs, vecs))

    def body(d, carry):
        other = lax.rem(spot + d, OCC_WAYS * VIR_WAYS)
        pltpu.make_async_remote_copy(
            src_ref=gm.at[spot], dst_ref=gm.at[spot], send_sem=g_send, recv_sem=g_recv,
            device_id={"occ": other // VIR_WAYS, "vir": lax.rem(other, VIR_WAYS)}, device_id_type=MESH,
        ).start()
        return carry

    lax.fori_loop(1, OCC_WAYS * VIR_WAYS, body, 0)
    wait_bytes(gm.at[pl.ds(0, OCC_WAYS * VIR_WAYS - 1)], g_recv)
    sums = [gm[j] for j in range(OCC_WAYS * VIR_WAYS)]
    while len(sums) > 1:
        sums = [a + b for a, b in zip(sums[0::2], sums[1::2])]
    coef_ref[3] = sums[0] * (1.0 / PAIRS)

    for step in range(2):
        wait_bytes(cvir.at[step, pl.ds(0, VIR_WAYS - 1)], cv_send.at[step])
        wait_bytes(cocc.at[step, pl.ds(0, OCC_WAYS - 1)], co_send.at[step])

        @pl.when(owner)
        def _():
            wait_bytes(part.at[step, pl.ds(0, TILES - 1)], rs_send.at[step])
            wait_bytes(rs.at[step, pl.ds(0, AUX_WAYS - 1)], ag_send.at[step])

        @pl.when(jnp.logical_not(owner))
        def _():
            wait_bytes(part.at[step], rs_send.at[step])

    wait_bytes(gm.at[pl.ds(0, OCC_WAYS * VIR_WAYS - 1)], g_send)


def finish(small_ref, resid_ref, coef_ref, next_ref):
    row, lane = iotas()
    lower = factor(small_ref[3])
    for k in range(3):
        coef_ref[k] = small_ref[k][:, :NV]
    coef_ref[3] = jnp.where(lane >= row, lower, 0.0)[:, :NV]
    for i in range(ROWS):
        next_ref[i] = apply(lower, resid_ref[i], NV)


def on_device(start_block, factors, eps_occ, eps_vir):
    tile_shape = (NV, LANES)
    dma = pltpu.SemaphoreType.DMA
    anywhere = pl.BlockSpec(memory_space=pltpu.MemorySpace.HBM)
    vmem = pl.BlockSpec(memory_space=pltpu.MemorySpace.VMEM)
    small, resid = pl.pallas_call(
        kernel,
        out_shape=(
            pltpu.VMEM((4,) + tile_shape, f32),
            pltpu.VMEM((ROWS,) + tile_shape, f32),
        ),
        in_specs=[anywhere] * 4,
        out_specs=(vmem, vmem),
        scratch_shapes=[
            pltpu.VMEM((ROWS,) + tile_shape, f32),
            pltpu.VMEM((2, ROWS, DEPTH, LANES), bf16),
            pltpu.SMEM((ROWS,), f32),
            pltpu.VMEM((1, LANES), f32),
            pltpu.VMEM((ROWS,) + tile_shape, f32),
            pltpu.VMEM((ROWS,) + tile_shape, f32),
            pltpu.VMEM((ROWS,) + tile_shape, f32),
            pltpu.VMEM((4,) + tile_shape, f32),
            pltpu.VMEM((2, VIR_WAYS, 5) + tile_shape, f32),
            pltpu.VMEM((2, OCC_WAYS, 5) + tile_shape, f32),
            pltpu.VMEM((2, TILES) + tile_shape, f32),
            pltpu.VMEM((2, AUX_WAYS) + tile_shape, f32),
            pltpu.VMEM((2, TILES) + tile_shape, f32),
            pltpu.VMEM((2,) + tile_shape, f32),
            pltpu.VMEM((OCC_WAYS * VIR_WAYS,) + tile_shape, f32),
            dma((3,)), dma((ROWS // GROUP,)),
            dma((2,)), dma((2,)), dma((2,)), dma((2,)),
            dma((2,)), dma((2,)), dma((2,)), dma((2,)),
            dma, dma,
        ],
        compiler_params=pltpu.CompilerParams(
            collective_id=0, has_side_effects=True, vmem_limit_bytes=60 * 1024 * 1024
        ),
        cost_estimate=pl.CostEstimate(flops=200_000_000, bytes_accessed=3_000_000, transcendentals=0),
    )(
        start_block.transpose(1, 0, 2),
        factors.transpose(0, 2, 1, 3),
        eps_occ,
        eps_vir.reshape(1, LANES),
    )
    coefs, block = pl.pallas_call(
        finish,
        out_shape=(
            jax.ShapeDtypeStruct((4, NV, NV), f32),
            jax.ShapeDtypeStruct((ROWS,) + tile_shape, f32),
        ),
        in_specs=[vmem] * 2,
        out_specs=(vmem, vmem),
        cost_estimate=pl.CostEstimate(flops=400_000, bytes_accessed=200_000, transcendentals=0),
    )(small, resid)
    return coefs, block.transpose(1, 0, 2)


def solution(mesh):
    placed = (P(None, "occ", "vir"), P(None, "aux", "occ", "vir"), P("occ"), P("vir"))
    return jax.shard_map(
        on_device,
        mesh=mesh,
        in_specs=placed,
        out_specs=(P(), P(None, "occ", "vir")),
        check_vma=False,
    )
```

profile of v0, /device:TPU:1, one launch (start us, length us, event | category | flops | bytes accessed | tf_op | source)
XLA Modules:
  0.0 79.5 jit_solution(12830375259646416717)
XLA Ops:
  0.6 75.4 %shard_map.59 = (f32[4,8,128]{2,1,0:T(8,128)S(1)}, f32[20,8,128]{2,1,0:T(8,128)S(1)}) custom-call(f32[20,8,128]{2,1,0:T(8,128)} %bitcast.5, bf16[2,20,256,128]{3,2,1,0:T(8,128)(2,1)} %bitcast.4, f32[20]{0:T(128)} %occ_hbm.1, f32[1,128]{1,0:T(1,128)} %bitcast.6), custom_call_target="tpu_custom_call" | custom-call | flops 200000000 | bytes 3000000 | tf_op jit(solution)/shard_map/pallas_call | solution.py:381
  76.0 0.0 copy-start
  76.0 0.6 copy-done
  76.6 0.0 copy-start.1
  76.6 0.6 copy-done.1
  77.2 2.3 %shard_map.60 = (f32[4,8,8]{2,1,0:T(8,128)}, f32[20,8,128]{2,1,0:T(8,128)}) custom-call(f32[4,8,128]{2,1,0:T(8,128)} %copy-done.1, f32[20,8,128]{2,1,0:T(8,128)} %copy-done), custom_call_target="tpu_custom_call" | custom-call | flops 400000 | bytes 200000 | tf_op jit(solution)/shard_map/pallas_call | solution.py:420
Async XLA Ops:
  76.0 0.6 copy-start
  76.6 0.6 copy-start.1
where the time goes:
time: 79.8 us; the launch traced here: 79.5 us
  Pallas kernels  77.7 us (97%)
  local copies, waits for them, and re-layouts  1.21 us (2%)
    pallas_call x1, Pallas kernels, on_device(): pl.pallas_call(kernel, out_shape=(pltpu.VMEM((4,) + tile_shape, f32), plt...  75.4 us
    pallas_call x1, Pallas kernels, on_device(): pl.pallas_call(finish, out_shape=(jax.ShapeDtypeStruct((4, NV, NV), f32),...  2.32 us

commit v1 on v0

--- a/solution.py
+++ b/solution.py
@@ -5,11 +5,12 @@
 from jax.experimental.pallas import tpu as pltpu
 from jax.sharding import PartitionSpec as P
 
-AUX_WAYS, OCC_WAYS, VIR_WAYS = 32, 4, 4
+OCC_WAYS, VIR_WAYS = 4, 4
 NV, ROWS, LANES, DEPTH = 8, 20, 128, 256
 PAIRS = 40960
 TILES = ROWS + 1
-STRIDE, UNSTRIDE = 3, 11
+NEAR, BLOCKS, Z, SHARE = 8, 4, 16, 3
+OWNERS = TILES // SHARE
 GROUP = 4
 MESH = pl.DeviceIdType.MESH
 f32, bf16 = jnp.float32, jnp.bfloat16
@@ -75,21 +76,36 @@
     start_hbm, fac_hbm, occ_hbm, vir_hbm,
     coef_ref, resid_ref,
     start, fac, eocc, evir, q1, q2, r1, xhat,
-    cvir, cocc, part, rs, ag, mine, gm,
+    cvir, cocc, part, rs, cx, ag, gm,
     in_sem, fac_sem, cv_send, cv_recv, co_send, co_recv,
-    rs_send, rs_recv, ag_send, ag_recv, g_send, g_recv,
+    rs_send, rs_recv, cx_send, cx_recv, ag_send, ag_recv, g_send, g_recv,
 ):
     aux = lax.axis_index("aux")
     occ = lax.axis_index("occ")
     vir = lax.axis_index("vir")
     spot = occ * VIR_WAYS + vir
     core = lax.rem(vir, 2)
-
-    def tile_of(device):
-        return lax.rem((device + core) * UNSTRIDE, AUX_WAYS)
-
-    tile = tile_of(aux)
-    owner = tile < TILES
+    side = aux // Z
+    block = lax.rem(aux, Z) // BLOCKS
+    place = lax.rem(aux, BLOCKS)
+    role = lax.rem(side * BLOCKS + place + BLOCKS * core, NEAR)
+    owner = role < OWNERS
+    own = pl.ds(role * SHARE, SHARE)
+
+    def near(other):
+        spot_of = lax.rem(other + BLOCKS * core, NEAR)
+        return {"aux": (spot_of // BLOCKS) * Z + block * BLOCKS + lax.rem(spot_of, BLOCKS)}
+
+    def far(d):
+        return {"aux": side * Z + lax.rem(block + d, BLOCKS) * BLOCKS + place}
+
+    def mate(d):
+        other = lax.rem(spot + d, OCC_WAYS * VIR_WAYS)
+        return {"occ": other // VIR_WAYS, "vir": lax.rem(other, VIR_WAYS)}
+
+    peers = [near(lax.rem(role + d, NEAR)) for d in range(1, NEAR)]
+    crosses = [far(d) for d in range(1, BLOCKS)]
+    mates = [mate(d) for d in range(1, OCC_WAYS * VIR_WAYS)]
 
     loads = [
         pltpu.make_async_copy(start_hbm, start, in_sem.at[0]),
@@ -107,22 +123,9 @@
 
     barrier = pltpu.get_barrier_semaphore()
 
-    def greet_aux(d, carry):
-        pl.semaphore_signal(
-            barrier, inc=1, device_id={"aux": lax.rem(aux + d, AUX_WAYS)}, device_id_type=MESH
-        )
-        return carry
-
-    def greet_spot(d, carry):
-        other = lax.rem(spot + d, OCC_WAYS * VIR_WAYS)
-        pl.semaphore_signal(
-            barrier, inc=1,
-            device_id={"occ": other // VIR_WAYS, "vir": lax.rem(other, VIR_WAYS)}, device_id_type=MESH,
-        )
-        return carry
-
-    lax.fori_loop(1, AUX_WAYS, greet_aux, 0)
-    lax.fori_loop(1, OCC_WAYS * VIR_WAYS, greet_spot, 0)
+    greeted = mates + peers + crosses
+    for device in greeted:
+        pl.semaphore_signal(barrier, inc=1, device_id=device, device_id_type=MESH)
 
     for load in loads:
         load.wait()
@@ -152,7 +155,7 @@
         for index, value in enumerate(tiles):
             cvir[step, vir, index] = value
         if first:
-            pl.semaphore_wait(barrier, AUX_WAYS - 1 + OCC_WAYS * VIR_WAYS - 1)
+            pl.semaphore_wait(barrier, len(greeted))
         for d in range(1, VIR_WAYS):
             pltpu.make_async_remote_copy(
                 src_ref=cvir.at[step, vir], dst_ref=cvir.at[step, vir],
@@ -178,47 +181,26 @@
             for index in range(count)
         ]
 
-    def both_ways(action):
-        def body(d, carry):
-            action(d)
-            action(AUX_WAYS - d)
-            return carry
-
-        lax.fori_loop(1, AUX_WAYS // 2, body, 0)
-        action(AUX_WAYS // 2)
-
-    def send_tile(step, t, target):
+    def send(source, target, sems, device):
         pltpu.make_async_remote_copy(
-            src_ref=part.at[step, t], dst_ref=rs.at[step, aux],
-            send_sem=rs_send.at[step], recv_sem=rs_recv.at[step],
-            device_id={"aux": target}, device_id_type=MESH,
+            src_ref=source, dst_ref=target, send_sem=sems[0], recv_sem=sems[1],
+            device_id=device, device_id_type=MESH,
         ).start()
 
-    def send_rows(step):
-        def action(d):
-            target = lax.rem(aux + d, AUX_WAYS)
-            t = tile_of(target)
-
-            @pl.when(t < ROWS)
+    def scatter(step):
+        for d in range(1, NEAR):
+            other = lax.rem(role + d, NEAR)
+
+            @pl.when(other < OWNERS)
             def _():
-                send_tile(step, t, target)
-
-        both_ways(action)
-
-        @pl.when(tile < ROWS)
+                send(
+                    part.at[step, pl.ds(other * SHARE, SHARE)], rs.at[step, role],
+                    (rs_send.at[step], rs_recv.at[step]), peers[d - 1],
+                )
+
+        @pl.when(owner)
         def _():
-            rs[step, aux] = part[step, tile]
-
-    def send_small(step):
-        target = lax.rem(ROWS * STRIDE - core, AUX_WAYS)
-
-        @pl.when(target != aux)
-        def _():
-            send_tile(step, ROWS, target)
-
-        @pl.when(target == aux)
-        def _():
-            rs[step, aux] = part[step, ROWS]
+            rs[step, role] = part[step, own]
 
     def back(step, sums):
         scaled = [
@@ -236,34 +218,43 @@
             both = merge(both)
             part[step, i] = both[:, :LANES]
             part[step, i + 1] = both[:, LANES:]
-        send_rows(step)
-
-    def spread(step, lower, extra):
+        scatter(step)
+
+    def spread(step, lower, turned, extra):
         @pl.when(owner)
         def _():
-            wait_bytes(rs.at[step, pl.ds(0, AUX_WAYS - 1)], rs_recv.at[step])
-            sums = [rs[step, j] for j in range(AUX_WAYS)]
+            wait_bytes(rs.at[step, pl.ds(0, NEAR - 1)], rs_recv.at[step])
+            sums = [rs[step, j] for j in range(NEAR)]
             while len(sums) > 1:
                 sums = [a + b for a, b in zip(sums[0::2], sums[1::2])]
-
-            @pl.when(tile < ROWS)
+            cx[step, block] = sums[0]
+            for d in range(1, BLOCKS):
+                send(
+                    cx.at[step, block], cx.at[step, block],
+                    (cx_send.at[step], cx_recv.at[step]), crosses[d - 1],
+                )
+            wait_bytes(cx.at[step, pl.ds(0, BLOCKS - 1)], cx_recv.at[step])
+            total = (cx[step, 0] + cx[step, 1]) + (cx[step, 2] + cx[step, 3])
+            for k in range(SHARE - 1):
+                ag[step, role * SHARE + k] = apply(lower, total[k], NV)
+            last = role * SHARE + SHARE - 1
+
+            @pl.when(role < OWNERS - 1)
             def _():
-                mine[step] = apply(lower, sums[0], NV)
-
-            @pl.when(tile == ROWS)
+                ag[step, last] = apply(lower, total[SHARE - 1], NV)
+
+            @pl.when(role == OWNERS - 1)
             def _():
-                mine[step] = (sums[0] + extra) * (1.0 / PAIRS)
-
-            def action(d):
-                pltpu.make_async_remote_copy(
-                    src_ref=mine.at[step], dst_ref=ag.at[step, tile],
-                    send_sem=ag_send.at[step], recv_sem=ag_recv.at[step],
-                    device_id={"aux": lax.rem(aux + d, AUX_WAYS)}, device_id_type=MESH,
-                ).start()
-
-            both_ways(action)
-            ag[step, tile] = mine[step]
-            wait_bytes(ag.at[step, pl.ds(0, TILES - 1)], ag_recv.at[step])
+                half = apply(lower, (total[SHARE - 1] + extra) * (1.0 / PAIRS), NV)
+                whole = apply(half, turned)
+                ag[step, last] = jnp.where(lane < NV, whole, half)
+
+            for device in peers:
+                send(
+                    ag.at[step, own], ag.at[step, own],
+                    (ag_send.at[step], ag_recv.at[step]), device,
+                )
+            wait_bytes(ag.at[step, pl.ds(0, TILES - SHARE)], ag_recv.at[step])
 
         @pl.when(jnp.logical_not(owner))
         def _():
@@ -283,23 +274,23 @@
     row, lane = iotas()
     weights = [2.0, 2.0, -1.0, -1.0]
 
+    def turn(lower):
+        return wide(small(jnp.where(lane == row, 1.0, 0.0)[:, :NV], lower[:, NV:2 * NV]))
+
     vecs = [start[i] for i in range(ROWS)]
     shifted = [vecs[i] * delta(i) for i in range(ROWS)]
     grams = columns(products(vecs, vecs) + products(vecs, shifted))
     sums = contract(vecs, True)
     *sums, grams = sum_group(0, sums + [grams], True)
+    part[0, ROWS] = columns(products([w * v for w, v in zip(weights, sums)], sums))
     back(0, sums)
     lower = factor(grams * (1.0 / PAIRS))
-    inverse = lower[:, NV:2 * NV]
-    hats = [apply(lower, value, NV) for value in sums]
     for index in range(4):
-        xhat[index] = hats[index]
-    part[0, ROWS] = columns(products([w * hat for w, hat in zip(weights, hats)], hats))
-    send_small(0)
-    middle = small(small(inverse, grams[:, NV:2 * NV]), inverse)
+        xhat[index] = apply(lower, sums[index], NV)
     for i in range(ROWS):
         q1[i] = apply(lower, start[i], NV)
-    spread(0, lower, wide(middle))
+    extra = jnp.where(lane < NV, pltpu.roll(grams, LANES - NV, 1), 0.0)
+    spread(0, lower, turn(lower), extra)
     proj = ag[0, ROWS]
     coef_ref[0] = proj
     for i in range(ROWS):
@@ -311,19 +302,15 @@
     grams = columns(products(vecs, vecs) + products(vecs, shifted) + products(vecs, moved))
     sums = contract(vecs, False)
     *sums, grams = sum_group(1, sums + [grams], False)
+    scaled = [w * v for w, v in zip(weights, sums)]
+    part[1, ROWS] = columns(products(scaled, sums) + products(scaled, [xhat[k] for k in range(4)]))
     back(1, sums)
     lower = factor(grams * (1.0 / PAIRS))
-    inverse = lower[:, NV:2 * NV]
-    hats = [apply(lower, value, NV) for value in sums]
-    scaled = [w * hat for w, hat in zip(weights, hats)]
-    part[1, ROWS] = columns(products(scaled, hats) + products(scaled, [xhat[k] for k in range(4)]))
-    send_small(1)
-    middle = small(small(inverse, grams[:, NV:2 * NV]), inverse)
-    across = apply(lower, grams[:, 2 * NV:3 * NV], NV)
     coef_ref[1] = jnp.where(lane >= row, lower, 0.0)
     for i in range(ROWS):
         q2[i] = apply(lower, r1[i], NV)
-    spread(1, lower, wide(jnp.concatenate([middle, across], axis=1)))
+    extra = jnp.where(lane < 2 * NV, pltpu.roll(grams, LANES - NV, 1), 0.0)
+    spread(1, lower, turn(lower), extra)
     proj = ag[1, ROWS]
     coef_ref[2] = proj
     for i in range(ROWS):
@@ -332,15 +319,8 @@
     vecs = [resid_ref[i] for i in range(ROWS)]
     gm[spot] = columns(products(vecs, vecs))
 
-    def body(d, carry):
-        other = lax.rem(spot + d, OCC_WAYS * VIR_WAYS)
-        pltpu.make_async_remote_copy(
-            src_ref=gm.at[spot], dst_ref=gm.at[spot], send_sem=g_send, recv_sem=g_recv,
-            device_id={"occ": other // VIR_WAYS, "vir": lax.rem(other, VIR_WAYS)}, device_id_type=MESH,
-        ).start()
-        return carry
-
-    lax.fori_loop(1, OCC_WAYS * VIR_WAYS, body, 0)
+    for device in mates:
+        send(gm.at[spot], gm.at[spot], (g_send, g_recv), device)
     wait_bytes(gm.at[pl.ds(0, OCC_WAYS * VIR_WAYS - 1)], g_recv)
     sums = [gm[j] for j in range(OCC_WAYS * VIR_WAYS)]
     while len(sums) > 1:
@@ -353,8 +333,9 @@
 
         @pl.when(owner)
         def _():
-            wait_bytes(part.at[step, pl.ds(0, TILES - 1)], rs_send.at[step])
-            wait_bytes(rs.at[step, pl.ds(0, AUX_WAYS - 1)], ag_send.at[step])
+            wait_bytes(part.at[step, pl.ds(0, TILES - SHARE)], rs_send.at[step])
+            wait_bytes(cx.at[step, pl.ds(0, BLOCKS - 1)], cx_send.at[step])
+            wait_bytes(rs.at[step, pl.ds(0, NEAR - 1)], ag_send.at[step])
 
         @pl.when(jnp.logical_not(owner))
         def _():
@@ -398,13 +379,13 @@
             pltpu.VMEM((2, VIR_WAYS, 5) + tile_shape, f32),
             pltpu.VMEM((2, OCC_WAYS, 5) + tile_shape, f32),
             pltpu.VMEM((2, TILES) + tile_shape, f32),
-            pltpu.VMEM((2, AUX_WAYS) + tile_shape, f32),
+            pltpu.VMEM((2, NEAR, SHARE) + tile_shape, f32),
+            pltpu.VMEM((2, BLOCKS, SHARE) + tile_shape, f32),
             pltpu.VMEM((2, TILES) + tile_shape, f32),
-            pltpu.VMEM((2,) + tile_shape, f32),
             pltpu.VMEM((OCC_WAYS * VIR_WAYS,) + tile_shape, f32),
             dma((3,)), dma((ROWS // GROUP,)),
             dma((2,)), dma((2,)), dma((2,)), dma((2,)),
-            dma((2,)), dma((2,)), dma((2,)), dma((2,)),
+            dma((2,)), dma((2,)), dma((2,)), dma((2,)), dma((2,)), dma((2,)),
             dma, dma,
         ],
         compiler_params=pltpu.CompilerParams(
@@ -425,6 +406,7 @@
         ),
         in_specs=[vmem] * 2,
         out_specs=(vmem, vmem),
+        compiler_params=pltpu.CompilerParams(vmem_limit_bytes=4 * 1024 * 1024),
         cost_estimate=pl.CostEstimate(flops=400_000, bytes_accessed=200_000, transcendentals=0),
     )(small, resid)
     return coefs, block.transpose(1, 0, 2)

time: 79.8 us -> 74.3 us (0.931)
  Pallas kernels: 77.7 us -> 73.5 us
  local copies, waits for them, and re-layouts: 1.21 us -> 0 us
    pallas_call x1, Pallas kernels: 75.4 us -> 72.1 us  [on_device(): pl.pallas_call(kernel, out_shape=(pltpu.VMEM((4,) + tile_shape, f32), plt...]
    unnamed x4 -> x0, local copies, waits for them, and re-layouts: 1.21 us -> none
    pallas_call x1, Pallas kernels: 2.32 us -> 1.41 us  [on_device(): pl.pallas_call(finish, out_shape=(jax.ShapeDtypeStruct((4, NV, NV), f32),...]
where the time goes in v1:
time: 74.3 us; the launch traced here: 74.1 us
  Pallas kernels  73.5 us (99%)
    pallas_call x1, Pallas kernels, on_device(): pl.pallas_call(kernel, out_shape=(pltpu.VMEM((4,) + tile_shape, f32), plt...  72.1 us

profile of v1, /device:TPU:1, one launch (start us, length us, event | category | flops | bytes accessed | tf_op | source)
XLA Modules:
  0.0 74.1 jit_solution(4112090182889909069)
XLA Ops:
  0.6 72.1 %shard_map.59 = (f32[4,8,128]{2,1,0:T(8,128)S(1)}, f32[20,8,128]{2,1,0:T(8,128)S(1)}) custom-call(f32[20,8,128]{2,1,0:T(8,128)} %bitcast.5, bf16[2,20,256,128]{3,2,1,0:T(8,128)(2,1)} %bitcast.4, f32[20]{0:T(128)} %occ_hbm.1, f32[1,128]{1,0:T(1,128)} %bitcast.6), custom_call_target="tpu_custom_call" | custom-call | flops 200000000 | bytes 3000000 | tf_op jit(solution)/shard_map/pallas_call | solution.py:362
  72.7 1.4 %shard_map.60 = (f32[4,8,8]{2,1,0:T(8,128)}, f32[20,8,128]{2,1,0:T(8,128)}) custom-call(f32[4,8,128]{2,1,0:T(8,128)S(1)} %get-tuple-element.6.small_ref, f32[20,8,128]{2,1,0:T(8,128)S(1)} %get-tuple-element.7.resid_ref), custom_call_target="tpu_custom_call" | custom-call | flops 400000 | bytes 200000 | tf_op jit(solution)/shard_map/pallas_call | solution.py:401

commit v2 on v1

--- a/solution.py
+++ b/solution.py
@@ -76,8 +76,8 @@
     start_hbm, fac_hbm, occ_hbm, vir_hbm,
     coef_ref, resid_ref,
     start, fac, eocc, evir, q1, q2, r1, xhat,
-    cvir, cocc, part, rs, cx, ag, gm,
-    in_sem, fac_sem, cv_send, cv_recv, co_send, co_recv,
+    cm, part, rs, cx, ag, gm,
+    in_sem, fac_sem, cm_send, cm_recv,
     rs_send, rs_recv, cx_send, cx_recv, ag_send, ag_recv, g_send, g_recv,
 ):
     aux = lax.axis_index("aux")
@@ -151,35 +151,20 @@
         pltpu.make_async_copy(ref, ref, sem).wait()
 
     def sum_group(step, tiles, first):
-        count = len(tiles)
         for index, value in enumerate(tiles):
-            cvir[step, vir, index] = value
+            cm[step, spot, index] = value
         if first:
             pl.semaphore_wait(barrier, len(greeted))
-        for d in range(1, VIR_WAYS):
-            pltpu.make_async_remote_copy(
-                src_ref=cvir.at[step, vir], dst_ref=cvir.at[step, vir],
-                send_sem=cv_send.at[step], recv_sem=cv_recv.at[step],
-                device_id={"vir": lax.rem(vir + d, VIR_WAYS)}, device_id_type=MESH,
-            ).start()
-        wait_bytes(cvir.at[step, pl.ds(0, VIR_WAYS - 1)], cv_recv.at[step])
-        for index in range(count):
-            cocc[step, occ, index] = (
-                (cvir[step, 0, index] + cvir[step, 1, index])
-                + (cvir[step, 2, index] + cvir[step, 3, index])
-            )
-        for d in range(1, OCC_WAYS):
-            pltpu.make_async_remote_copy(
-                src_ref=cocc.at[step, occ], dst_ref=cocc.at[step, occ],
-                send_sem=co_send.at[step], recv_sem=co_recv.at[step],
-                device_id={"occ": lax.rem(occ + d, OCC_WAYS)}, device_id_type=MESH,
-            ).start()
-        wait_bytes(cocc.at[step, pl.ds(0, OCC_WAYS - 1)], co_recv.at[step])
-        return [
-            (cocc[step, 0, index] + cocc[step, 1, index])
-            + (cocc[step, 2, index] + cocc[step, 3, index])
-            for index in range(count)
-        ]
+        for device in mates:
+            send(cm.at[step, spot], cm.at[step, spot], (cm_send.at[step], cm_recv.at[step]), device)
+        wait_bytes(cm.at[step, pl.ds(0, len(mates))], cm_recv.at[step])
+        out = []
+        for index in range(len(tiles)):
+            sums = [cm[step, j, index] for j in range(OCC_WAYS * VIR_WAYS)]
+            while len(sums) > 1:
+                sums = [a + b for a, b in zip(sums[0::2], sums[1::2])]
+            out.append(sums[0])
+        return out
 
     def send(source, target, sems, device):
         pltpu.make_async_remote_copy(
@@ -328,8 +313,7 @@
     coef_ref[3] = sums[0] * (1.0 / PAIRS)
 
     for step in range(2):
-        wait_bytes(cvir.at[step, pl.ds(0, VIR_WAYS - 1)], cv_send.at[step])
-        wait_bytes(cocc.at[step, pl.ds(0, OCC_WAYS - 1)], co_send.at[step])
+        wait_bytes(cm.at[step, pl.ds(0, len(mates))], cm_send.at[step])
 
         @pl.when(owner)
         def _():
@@ -376,15 +360,14 @@
             pltpu.VMEM((ROWS,) + tile_shape, f32),
             pltpu.VMEM((ROWS,) + tile_shape, f32),
             pltpu.VMEM((4,) + tile_shape, f32),
-            pltpu.VMEM((2, VIR_WAYS, 5) + tile_shape, f32),
-            pltpu.VMEM((2, OCC_WAYS, 5) + tile_shape, f32),
+            pltpu.VMEM((2, OCC_WAYS * VIR_WAYS, 5) + tile_shape, f32),
             pltpu.VMEM((2, TILES) + tile_shape, f32),
             pltpu.VMEM((2, NEAR, SHARE) + tile_shape, f32),
             pltpu.VMEM((2, BLOCKS, SHARE) + tile_shape, f32),
             pltpu.VMEM((2, TILES) + tile_shape, f32),
             pltpu.VMEM((OCC_WAYS * VIR_WAYS,) + tile_shape, f32),
             dma((3,)), dma((ROWS // GROUP,)),
-            dma((2,)), dma((2,)), dma((2,)), dma((2,)),
+            dma((2,)), dma((2,)),
             dma((2,)), dma((2,)), dma((2,)), dma((2,)), dma((2,)), dma((2,)),
             dma, dma,
         ],

time: 74.3 us -> 71.1 us (0.957)
  Pallas kernels: 73.5 us -> 70.3 us
    pallas_call x1, Pallas kernels: 72.1 us -> 68.9 us  [on_device(): pl.pallas_call(kernel, out_shape=(pltpu.VMEM((4,) + tile_shape, f32), plt...]
where the time goes in v2:
time: 71.1 us; the launch traced here: 70.9 us
  Pallas kernels  70.3 us (99%)
    pallas_call x1, Pallas kernels, on_device(): pl.pallas_call(kernel, out_shape=(pltpu.VMEM((4,) + tile_shape, f32), plt...  68.9 us

profile of v2, /device:TPU:1, one launch (start us, length us, event | category | flops | bytes accessed | tf_op | source)
XLA Modules:
  0.0 70.9 jit_solution(3107942455220357588)
XLA Ops:
  0.6 68.9 %shard_map.59 = (f32[4,8,128]{2,1,0:T(8,128)S(1)}, f32[20,8,128]{2,1,0:T(8,128)S(1)}) custom-call(f32[20,8,128]{2,1,0:T(8,128)} %bitcast.5, bf16[2,20,256,128]{3,2,1,0:T(8,128)(2,1)} %bitcast.4, f32[20]{0:T(128)} %occ_hbm.1, f32[1,128]{1,0:T(1,128)} %bitcast.6), custom_call_target="tpu_custom_call" | custom-call | flops 200000000 | bytes 3000000 | tf_op jit(solution)/shard_map/pallas_call | solution.py:346
  69.5 1.4 %shard_map.60 = (f32[4,8,8]{2,1,0:T(8,128)}, f32[20,8,128]{2,1,0:T(8,128)}) custom-call(f32[4,8,128]{2,1,0:T(8,128)S(1)} %get-tuple-element.6.small_ref, f32[20,8,128]{2,1,0:T(8,128)S(1)} %get-tuple-element.7.resid_ref), custom_call_target="tpu_custom_call" | custom-call | flops 400000 | bytes 200000 | tf_op jit(solution)/shard_map/pallas_call | solution.py:384

commit v3 on v2

--- a/solution.py
+++ b/solution.py
@@ -11,7 +11,7 @@
 TILES = ROWS + 1
 NEAR, BLOCKS, Z, SHARE = 8, 4, 16, 3
 OWNERS = TILES // SHARE
-GROUP = 4
+HALF = ROWS // 2
 MESH = pl.DeviceIdType.MESH
 f32, bf16 = jnp.float32, jnp.bfloat16
 
@@ -26,10 +26,16 @@
     return value[:NV] + value[NV:]
 
 
-def apply(matrix, value, first=0):
-    total = matrix[:, first:first + 1] * value[0:1, :]
+def columns_of(matrix, first=0):
+    return [
+        jnp.broadcast_to(matrix[:, first + m:first + m + 1], (NV, LANES)) for m in range(NV)
+    ]
+
+
+def apply(columns, value):
+    total = columns[0] * value[0:1, :]
     for m in range(1, NV):
-        total = total + matrix[:, first + m:first + m + 1] * value[m:m + 1, :]
+        total = total + columns[m] * value[m:m + 1, :]
     return total
 
 
@@ -62,20 +68,22 @@
     return out
 
 
-def products(lefts, rights):
-    sums = []
+def add_products(sums, lefts, right):
     for m in range(NV):
-        total = lefts[0] * rights[0][m:m + 1, :]
-        for left, right in zip(lefts[1:], rights[1:]):
-            total = total + left * right[m:m + 1, :]
-        sums.append(total)
+        row = right[m:m + 1, :]
+        for k, left in enumerate(lefts):
+            sums[k * NV + m] = sums[k * NV + m] + left * row
     return sums
+
+
+def zeros(count):
+    return [jnp.zeros((NV, LANES), f32) for _ in range(count)]
 
 
 def kernel(
     start_hbm, fac_hbm, occ_hbm, vir_hbm,
     coef_ref, resid_ref,
-    start, fac, eocc, evir, q1, q2, r1, xhat,
+    fac, eocc, evir, q,
     cm, part, rs, cx, ag, gm,
     in_sem, fac_sem, cm_send, cm_recv,
     rs_send, rs_recv, cx_send, cx_recv, ag_send, ag_recv, g_send, g_recv,
@@ -108,53 +116,81 @@
     mates = [mate(d) for d in range(1, OCC_WAYS * VIR_WAYS)]
 
     loads = [
-        pltpu.make_async_copy(start_hbm, start, in_sem.at[0]),
+        pltpu.make_async_copy(start_hbm, resid_ref, in_sem.at[0]),
         pltpu.make_async_copy(occ_hbm, eocc, in_sem.at[1]),
         pltpu.make_async_copy(vir_hbm, evir, in_sem.at[2]),
     ]
     fac_loads = [
         pltpu.make_async_copy(
-            fac_hbm.at[:, pl.ds(GROUP * c, GROUP)], fac.at[:, pl.ds(GROUP * c, GROUP)], fac_sem.at[c]
+            fac_hbm.at[:, pl.ds(HALF * c, HALF)], fac.at[:, pl.ds(HALF * c, HALF)], fac_sem.at[c]
         )
-        for c in range(ROWS // GROUP)
+        for c in range(2)
     ]
-    for load in loads + fac_loads:
+    for load in loads:
         load.start()
 
     barrier = pltpu.get_barrier_semaphore()
 
     greeted = mates + peers + crosses
-    for device in greeted:
+    for device in mates:
         pl.semaphore_signal(barrier, inc=1, device_id=device, device_id_type=MESH)
-
+    for load in fac_loads:
+        load.start()
+    for device in peers + crosses:
+        pl.semaphore_signal(barrier, inc=1, device_id=device, device_id_type=MESH)
+
+    for i in range(ROWS):
+        q[0, i] = jnp.zeros((NV, LANES), f32)
     for load in loads:
         load.wait()
 
     def delta(i):
         return evir[...] - eocc[i]
 
-    def contract(source, waits):
-        sums = [None, None]
-        for i in range(0, ROWS, 2):
-            if waits and i % GROUP == 0:
-                fac_loads[i // GROUP].wait()
-            left = jnp.concatenate([split(source[i]), split(source[i + 1])], axis=1)
-            for s in range(2):
-                right = jnp.concatenate([fac[s, i], fac[s, i + 1]], axis=1)
-                term = lax.dot_general(
-                    left, right, (((1,), (1,)), ((), ())), preferred_element_type=f32
-                )
-                sums[s] = term if sums[s] is None else sums[s] + term
-        return [merge(sums[s])[:, LANES * h:LANES * (h + 1)] for s in range(2) for h in range(2)]
+    def pairs(s, i):
+        return jnp.concatenate([fac[s, i], fac[s, i + 1]], axis=1)
+
+    def contract(step):
+        def body(half, carry):
+            @pl.when(step == 0)
+            def _():
+                pltpu.make_async_copy(
+                    fac_hbm.at[:, pl.ds(HALF * half, HALF)], fac.at[:, pl.ds(HALF * half, HALF)],
+                    fac_sem.at[half],
+                ).wait()
+
+            sums, grams = list(carry[:2]), list(carry[2:])
+            for k in range(0, HALF, 2):
+                i = half * HALF + k
+                left = []
+                for u in range(2):
+                    value = resid_ref[i + u]
+                    shift = delta(i + u)
+                    grams = add_products(grams, [value, shift * value, shift * q[step, i + u]], value)
+                    left.append(split(value))
+                left = jnp.concatenate(left, axis=1)
+                for s in range(2):
+                    sums[s] = sums[s] + lax.dot_general(
+                        left, pairs(s, i), (((1,), (1,)), ((), ())), preferred_element_type=f32
+                    )
+            return (*sums, *grams)
+
+        start = [jnp.zeros((2 * NV, DEPTH), f32) for _ in range(2)] + zeros(3 * NV)
+        out = lax.fori_loop(0, 2, body, tuple(start))
+        tiles = [merge(out[s])[:, LANES * h:LANES * (h + 1)] for s in range(2) for h in range(2)]
+        return tiles + [columns(out[2:])]
 
     def wait_bytes(ref, sem):
         pltpu.make_async_copy(ref, ref, sem).wait()
 
-    def sum_group(step, tiles, first):
+    def sum_group(step, tiles):
         for index, value in enumerate(tiles):
             cm[step, spot, index] = value
-        if first:
+
+        @pl.when(step == 0)
+        def _():
             pl.semaphore_wait(barrier, len(greeted))
+
         for device in mates:
             send(cm.at[step, spot], cm.at[step, spot], (cm_send.at[step], cm_recv.at[step]), device)
         wait_bytes(cm.at[step, pl.ds(0, len(mates))], cm_recv.at[step])
@@ -192,17 +228,22 @@
             split(jnp.concatenate([2.0 * sums[0], 2.0 * sums[1]], axis=1)),
             split(jnp.concatenate([-sums[2], -sums[3]], axis=1)),
         ]
-        for i in range(0, ROWS, 2):
-            both = None
-            for s in range(2):
-                right = jnp.concatenate([fac[s, i], fac[s, i + 1]], axis=1)
-                term = lax.dot_general(
-                    scaled[s], right, (((1,), (0,)), ((), ())), preferred_element_type=f32
-                )
-                both = term if both is None else both + term
-            both = merge(both)
-            part[step, i] = both[:, :LANES]
-            part[step, i + 1] = both[:, LANES:]
+
+        def body(half, carry):
+            for k in range(0, HALF, 2):
+                i = half * HALF + k
+                both = None
+                for s in range(2):
+                    term = lax.dot_general(
+                        scaled[s], pairs(s, i), (((1,), (0,)), ((), ())), preferred_element_type=f32
+                    )
+                    both = term if both is None else both + term
+                both = merge(both)
+                part[step, i] = both[:, :LANES]
+                part[step, i + 1] = both[:, LANES:]
+            return carry
+
+        lax.fori_loop(0, 2, body, 0)
         scatter(step)
 
     def spread(step, lower, turned, extra):
@@ -221,17 +262,17 @@
             wait_bytes(cx.at[step, pl.ds(0, BLOCKS - 1)], cx_recv.at[step])
             total = (cx[step, 0] + cx[step, 1]) + (cx[step, 2] + cx[step, 3])
             for k in range(SHARE - 1):
-                ag[step, role * SHARE + k] = apply(lower, total[k], NV)
+                ag[step, role * SHARE + k] = apply(lower, total[k])
             last = role * SHARE + SHARE - 1
 
             @pl.when(role < OWNERS - 1)
             def _():
-                ag[step, last] = apply(lower, total[SHARE - 1], NV)
+                ag[step, last] = apply(lower, total[SHARE - 1])
 
             @pl.when(role == OWNERS - 1)
             def _():
-                half = apply(lower, (total[SHARE - 1] + extra) * (1.0 / PAIRS), NV)
-                whole = apply(half, turned)
+                half = apply(lower, (total[SHARE - 1] + extra) * (1.0 / PAIRS))
+                whole = apply(columns_of(half), turned)
                 ag[step, last] = jnp.where(lane < NV, whole, half)
 
             for device in peers:
@@ -259,50 +300,61 @@
     row, lane = iotas()
     weights = [2.0, 2.0, -1.0, -1.0]
 
-    def turn(lower):
-        return wide(small(jnp.where(lane == row, 1.0, 0.0)[:, :NV], lower[:, NV:2 * NV]))
-
-    vecs = [start[i] for i in range(ROWS)]
-    shifted = [vecs[i] * delta(i) for i in range(ROWS)]
-    grams = columns(products(vecs, vecs) + products(vecs, shifted))
-    sums = contract(vecs, True)
-    *sums, grams = sum_group(0, sums + [grams], True)
-    part[0, ROWS] = columns(products([w * v for w, v in zip(weights, sums)], sums))
-    back(0, sums)
-    lower = factor(grams * (1.0 / PAIRS))
-    for index in range(4):
-        xhat[index] = apply(lower, sums[index], NV)
-    for i in range(ROWS):
-        q1[i] = apply(lower, start[i], NV)
-    extra = jnp.where(lane < NV, pltpu.roll(grams, LANES - NV, 1), 0.0)
-    spread(0, lower, turn(lower), extra)
-    proj = ag[0, ROWS]
-    coef_ref[0] = proj
-    for i in range(ROWS):
-        r1[i] = ag[0, i] + delta(i) * q1[i] - apply(proj, q1[i])
-
-    vecs = [r1[i] for i in range(ROWS)]
-    moved = [delta(i) * q1[i] for i in range(ROWS)]
-    shifted = [vecs[i] * delta(i) for i in range(ROWS)]
-    grams = columns(products(vecs, vecs) + products(vecs, shifted) + products(vecs, moved))
-    sums = contract(vecs, False)
-    *sums, grams = sum_group(1, sums + [grams], False)
-    scaled = [w * v for w, v in zip(weights, sums)]
-    part[1, ROWS] = columns(products(scaled, sums) + products(scaled, [xhat[k] for k in range(4)]))
-    back(1, sums)
-    lower = factor(grams * (1.0 / PAIRS))
-    coef_ref[1] = jnp.where(lane >= row, lower, 0.0)
-    for i in range(ROWS):
-        q2[i] = apply(lower, r1[i], NV)
-    extra = jnp.where(lane < 2 * NV, pltpu.roll(grams, LANES - NV, 1), 0.0)
-    spread(1, lower, turn(lower), extra)
-    proj = ag[1, ROWS]
-    coef_ref[2] = proj
-    for i in range(ROWS):
-        resid_ref[i] = ag[1, i] + delta(i) * q2[i] - apply(proj, q2[i]) - apply(proj, q1[i], NV)
-
-    vecs = [resid_ref[i] for i in range(ROWS)]
-    gm[spot] = columns(products(vecs, vecs))
+    def turned(value):
+        return wide(small(jnp.where(lane == row, 1.0, 0.0)[:, :NV], value))
+
+    def one_step(step, hats):
+        *sums, grams = sum_group(step, contract(step))
+        scaled = [w * v for w, v in zip(weights, sums)]
+        pieces = zeros(2 * NV)
+        for m in range(NV):
+            for k in range(4):
+                pieces[m] = pieces[m] + scaled[k] * sums[k][m:m + 1, :]
+                pieces[NV + m] = pieces[NV + m] + scaled[k] * hats[k][m:m + 1, :]
+        part[step, ROWS] = columns(pieces)
+        back(step, sums)
+
+        both = factor(grams * (1.0 / PAIRS))
+        coef_ref[lax.rem(2 * step + 3, 4)] = jnp.where(lane >= row, both, 0.0)
+        lower = columns_of(both, NV)
+        after = tuple(apply(lower, sums[k]) for k in range(4))
+
+        def turn_block(group, carry):
+            for k in range(4):
+                q[step + 1, group * 4 + k] = apply(lower, resid_ref[group * 4 + k])
+            return carry
+
+        lax.fori_loop(0, ROWS // 4, turn_block, 0)
+        extra = jnp.where(lane < NV, pltpu.roll(grams, LANES - NV, 1), 0.0)
+        extra = extra + pltpu.roll(turned(grams[:, 2 * NV:3 * NV]), NV, 1)
+        spread(step, lower, turned(both[:, NV:2 * NV]), extra)
+
+        proj = ag[step, ROWS]
+        coef_ref[2 * step] = proj
+        now, before = columns_of(proj), columns_of(proj, NV)
+
+        def take_away(half, carry):
+            for k in range(HALF):
+                i = half * HALF + k
+                block = q[step + 1, i]
+                resid_ref[i] = (
+                    ag[step, i] + delta(i) * block - apply(now, block) - apply(before, q[step, i])
+                )
+            return carry
+
+        lax.fori_loop(0, 2, take_away, 0)
+        return after
+
+    lax.fori_loop(0, 2, one_step, tuple(zeros(4)))
+
+    def last_products(half, sums):
+        sums = list(sums)
+        for k in range(HALF):
+            value = resid_ref[half * HALF + k]
+            sums = add_products(sums, [value], value)
+        return tuple(sums)
+
+    gm[spot] = columns(lax.fori_loop(0, 2, last_products, tuple(zeros(NV))))
 
     for device in mates:
         send(gm.at[spot], gm.at[spot], (g_send, g_recv), device)
@@ -331,11 +383,12 @@
 def finish(small_ref, resid_ref, coef_ref, next_ref):
     row, lane = iotas()
     lower = factor(small_ref[3])
+    inverse = columns_of(lower, NV)
     for k in range(3):
         coef_ref[k] = small_ref[k][:, :NV]
     coef_ref[3] = jnp.where(lane >= row, lower, 0.0)[:, :NV]
     for i in range(ROWS):
-        next_ref[i] = apply(lower, resid_ref[i], NV)
+        next_ref[i] = apply(inverse, resid_ref[i])
 
 
 def on_device(start_block, factors, eps_occ, eps_vir):
@@ -352,21 +405,17 @@
         in_specs=[anywhere] * 4,
         out_specs=(vmem, vmem),
         scratch_shapes=[
-            pltpu.VMEM((ROWS,) + tile_shape, f32),
             pltpu.VMEM((2, ROWS, DEPTH, LANES), bf16),
             pltpu.SMEM((ROWS,), f32),
             pltpu.VMEM((1, LANES), f32),
-            pltpu.VMEM((ROWS,) + tile_shape, f32),
-            pltpu.VMEM((ROWS,) + tile_shape, f32),
-            pltpu.VMEM((ROWS,) + tile_shape, f32),
-            pltpu.VMEM((4,) + tile_shape, f32),
+            pltpu.VMEM((3, ROWS) + tile_shape, f32),
             pltpu.VMEM((2, OCC_WAYS * VIR_WAYS, 5) + tile_shape, f32),
             pltpu.VMEM((2, TILES) + tile_shape, f32),
             pltpu.VMEM((2, NEAR, SHARE) + tile_shape, f32),
             pltpu.VMEM((2, BLOCKS, SHARE) + tile_shape, f32),
             pltpu.VMEM((2, TILES) + tile_shape, f32),
             pltpu.VMEM((OCC_WAYS * VIR_WAYS,) + tile_shape, f32),
-            dma((3,)), dma((ROWS // GROUP,)),
+            dma((3,)), dma((2,)),
             dma((2,)), dma((2,)),
             dma((2,)), dma((2,)), dma((2,)), dma((2,)), dma((2,)), dma((2,)),
             dma, dma,

time: 71.1 us -> 71.7 us (level)
  no operation moved by 1% of the time
where the time goes in v3:
time: 71.7 us; the launch traced here: 71.6 us
  Pallas kernels  71 us (99%)
    pallas_call x1, Pallas kernels, on_device(): pl.pallas_call(kernel, out_shape=(pltpu.VMEM((4,) + tile_shape, f32), plt...  69.5 us

profile of v3, /device:TPU:1, one launch (start us, length us, event | category | flops | bytes accessed | tf_op | source)
XLA Modules:
  0.0 71.6 jit_solution(2901399557106588041)
XLA Ops:
  0.6 69.5 %shard_map.59 = (f32[4,8,128]{2,1,0:T(8,128)S(1)}, f32[20,8,128]{2,1,0:T(8,128)S(1)}) custom-call(f32[20,8,128]{2,1,0:T(8,128)} %bitcast.5, bf16[2,20,256,128]{3,2,1,0:T(8,128)(2,1)} %bitcast.4, f32[20]{0:T(128)} %occ_hbm.1, f32[1,128]{1,0:T(1,128)} %bitcast.6), custom_call_target="tpu_custom_call" | custom-call | flops 200000000 | bytes 3000000 | tf_op jit(solution)/shard_map/pallas_call | solution.py:399
  70.2 1.4 %shard_map.60 = (f32[4,8,8]{2,1,0:T(8,128)}, f32[20,8,128]{2,1,0:T(8,128)}) custom-call(f32[4,8,128]{2,1,0:T(8,128)S(1)} %get-tuple-element.6.small_ref, f32[20,8,128]{2,1,0:T(8,128)S(1)} %get-tuple-element.7.resid_ref), custom_call_target="tpu_custom_call" | custom-call | flops 400000 | bytes 200000 | tf_op jit(solution)/shard_map/pallas_call | solution.py:433

commit v4 on v2

--- a/solution.py
+++ b/solution.py
@@ -11,6 +11,7 @@
 TILES = ROWS + 1
 NEAR, BLOCKS, Z, SHARE = 8, 4, 16, 3
 OWNERS = TILES // SHARE
+CHIPS = 8
 GROUP = 4
 MESH = pl.DeviceIdType.MESH
 f32, bf16 = jnp.float32, jnp.bfloat16
@@ -76,8 +77,8 @@
     start_hbm, fac_hbm, occ_hbm, vir_hbm,
     coef_ref, resid_ref,
     start, fac, eocc, evir, q1, q2, r1, xhat,
-    cm, part, rs, cx, ag, gm,
-    in_sem, fac_sem, cm_send, cm_recv,
+    cc, cm, part, rs, cx, ag, gm,
+    in_sem, fac_sem, cc_send, cc_recv, cm_send, cm_recv,
     rs_send, rs_recv, cx_send, cx_recv, ag_send, ag_recv, g_send, g_recv,
 ):
     aux = lax.axis_index("aux")
@@ -85,6 +86,7 @@
     vir = lax.axis_index("vir")
     spot = occ * VIR_WAYS + vir
     core = lax.rem(vir, 2)
+    chip = occ * 2 + vir // 2
     side = aux // Z
     block = lax.rem(aux, Z) // BLOCKS
     place = lax.rem(aux, BLOCKS)
@@ -118,14 +120,17 @@
         )
         for c in range(ROWS // GROUP)
     ]
-    for load in loads + fac_loads:
+    for load in loads:
         load.start()
 
     barrier = pltpu.get_barrier_semaphore()
 
-    greeted = mates + peers + crosses
-    for device in greeted:
+    greeted = crosses + peers + mates
+    for index, device in enumerate(greeted):
         pl.semaphore_signal(barrier, inc=1, device_id=device, device_id_type=MESH)
+        if index == len(crosses) - 1:
+            for load in fac_loads:
+                load.start()
 
     for load in loads:
         load.wait()
@@ -152,15 +157,26 @@
 
     def sum_group(step, tiles, first):
         for index, value in enumerate(tiles):
-            cm[step, spot, index] = value
+            cc[step, core, index] = value
         if first:
             pl.semaphore_wait(barrier, len(greeted))
-        for device in mates:
-            send(cm.at[step, spot], cm.at[step, spot], (cm_send.at[step], cm_recv.at[step]), device)
-        wait_bytes(cm.at[step, pl.ds(0, len(mates))], cm_recv.at[step])
+        send(
+            cc.at[step, core], cc.at[step, core], (cc_send.at[step], cc_recv.at[step]),
+            {"vir": vir + 1 - 2 * core},
+        )
+        wait_bytes(cc.at[step, 0], cc_recv.at[step])
+        for index in range(len(tiles)):
+            cm[step, chip, index] = cc[step, 0, index] + cc[step, 1, index]
+        for d in range(1, CHIPS):
+            other = lax.rem(chip + d, CHIPS)
+            send(
+                cm.at[step, chip], cm.at[step, chip], (cm_send.at[step], cm_recv.at[step]),
+                {"occ": other // 2, "vir": lax.rem(other, 2) * 2 + core},
+            )
+        wait_bytes(cm.at[step, pl.ds(0, CHIPS - 1)], cm_recv.at[step])
         out = []
         for index in range(len(tiles)):
-            sums = [cm[step, j, index] for j in range(OCC_WAYS * VIR_WAYS)]
+            sums = [cm[step, j, index] for j in range(CHIPS)]
             while len(sums) > 1:
                 sums = [a + b for a, b in zip(sums[0::2], sums[1::2])]
             out.append(sums[0])
@@ -313,7 +329,8 @@
     coef_ref[3] = sums[0] * (1.0 / PAIRS)
 
     for step in range(2):
-        wait_bytes(cm.at[step, pl.ds(0, len(mates))], cm_send.at[step])
+        wait_bytes(cc.at[step, 0], cc_send.at[step])
+        wait_bytes(cm.at[step, pl.ds(0, CHIPS - 1)], cm_send.at[step])
 
         @pl.when(owner)
         def _():
@@ -360,14 +377,15 @@
             pltpu.VMEM((ROWS,) + tile_shape, f32),
             pltpu.VMEM((ROWS,) + tile_shape, f32),
             pltpu.VMEM((4,) + tile_shape, f32),
-            pltpu.VMEM((2, OCC_WAYS * VIR_WAYS, 5) + tile_shape, f32),
+            pltpu.VMEM((2, 2, 5) + tile_shape, f32),
+            pltpu.VMEM((2, CHIPS, 5) + tile_shape, f32),
             pltpu.VMEM((2, TILES) + tile_shape, f32),
             pltpu.VMEM((2, NEAR, SHARE) + tile_shape, f32),
             pltpu.VMEM((2, BLOCKS, SHARE) + tile_shape, f32),
             pltpu.VMEM((2, TILES) + tile_shape, f32),
             pltpu.VMEM((OCC_WAYS * VIR_WAYS,) + tile_shape, f32),
             dma((3,)), dma((ROWS // GROUP,)),
-            dma((2,)), dma((2,)),
+            dma((2,)), dma((2,)), dma((2,)), dma((2,)),
             dma((2,)), dma((2,)), dma((2,)), dma((2,)), dma((2,)), dma((2,)),
             dma, dma,
         ],

time: 71.1 us -> 71.1 us (level)
  no operation moved by 1% of the time
where the time goes in v4:
time: 71.1 us; the launch traced here: 70.9 us
  Pallas kernels  70.3 us (99%)
    pallas_call x1, Pallas kernels, on_device(): pl.pallas_call(kernel, out_shape=(pltpu.VMEM((4,) + tile_shape, f32), plt...  68.9 us

profile of v4, /device:TPU:1, one launch (start us, length us, event | category | flops | bytes accessed | tf_op | source)
XLA Modules:
  0.0 70.9 jit_solution(17643573447547009897)
XLA Ops:
  0.6 68.9 %shard_map.59 = (f32[4,8,128]{2,1,0:T(8,128)S(1)}, f32[20,8,128]{2,1,0:T(8,128)S(1)}) custom-call(f32[20,8,128]{2,1,0:T(8,128)} %bitcast.5, bf16[2,20,256,128]{3,2,1,0:T(8,128)(2,1)} %bitcast.4, f32[20]{0:T(128)} %occ_hbm.1, f32[1,128]{1,0:T(1,128)} %bitcast.6), custom_call_target="tpu_custom_call" | custom-call | flops 200000000 | bytes 3000000 | tf_op jit(solution)/shard_map/pallas_call | solution.py:363
  69.5 1.4 %shard_map.60 = (f32[4,8,8]{2,1,0:T(8,128)}, f32[20,8,128]{2,1,0:T(8,128)}) custom-call(f32[4,8,128]{2,1,0:T(8,128)S(1)} %get-tuple-element.6.small_ref, f32[20,8,128]{2,1,0:T(8,128)S(1)} %get-tuple-element.7.resid_ref), custom_call_target="tpu_custom_call" | custom-call | flops 400000 | bytes 200000 | tf_op jit(solution)/shard_map/pallas_call | solution.py:402

commit v5 on v4

--- a/solution.py
+++ b/solution.py
@@ -11,6 +11,7 @@
 TILES = ROWS + 1
 NEAR, BLOCKS, Z, SHARE = 8, 4, 16, 3
 OWNERS = TILES // SHARE
+SHIFT = 2
 CHIPS = 8
 GROUP = 4
 MESH = pl.DeviceIdType.MESH
@@ -88,18 +89,23 @@
     core = lax.rem(vir, 2)
     chip = occ * 2 + vir // 2
     side = aux // Z
-    block = lax.rem(aux, Z) // BLOCKS
-    place = lax.rem(aux, BLOCKS)
+    along = lax.rem(lax.rem(aux, Z) + SHIFT * core, Z)
+    block = along // BLOCKS
+    place = lax.rem(along, BLOCKS)
     role = lax.rem(side * BLOCKS + place + BLOCKS * core, NEAR)
     owner = role < OWNERS
     own = pl.ds(role * SHARE, SHARE)
 
+    def at(side_of, block_of, place_of):
+        z = lax.rem(block_of * BLOCKS + place_of + Z - SHIFT * core, Z)
+        return {"aux": side_of * Z + z}
+
     def near(other):
         spot_of = lax.rem(other + BLOCKS * core, NEAR)
-        return {"aux": (spot_of // BLOCKS) * Z + block * BLOCKS + lax.rem(spot_of, BLOCKS)}
+        return at(spot_of // BLOCKS, block, lax.rem(spot_of, BLOCKS))
 
     def far(d):
-        return {"aux": side * Z + lax.rem(block + d, BLOCKS) * BLOCKS + place}
+        return at(side, lax.rem(block + d, BLOCKS), place)
 
     def mate(d):
         other = lax.rem(spot + d, OCC_WAYS * VIR_WAYS)
@@ -293,7 +299,7 @@
     extra = jnp.where(lane < NV, pltpu.roll(grams, LANES - NV, 1), 0.0)
     spread(0, lower, turn(lower), extra)
     proj = ag[0, ROWS]
-    coef_ref[0] = proj
+    proj1 = proj
     for i in range(ROWS):
         r1[i] = ag[0, i] + delta(i) * q1[i] - apply(proj, q1[i])
 
@@ -313,12 +319,16 @@
     extra = jnp.where(lane < 2 * NV, pltpu.roll(grams, LANES - NV, 1), 0.0)
     spread(1, lower, turn(lower), extra)
     proj = ag[1, ROWS]
-    coef_ref[2] = proj
     for i in range(ROWS):
         resid_ref[i] = ag[1, i] + delta(i) * q2[i] - apply(proj, q2[i]) - apply(proj, q1[i], NV)
 
     vecs = [resid_ref[i] for i in range(ROWS)]
-    gm[spot] = columns(products(vecs, vecs))
+    grams = columns(products(vecs, vecs))
+    grams = jnp.where(jnp.logical_and(lane >= NV, lane < 2 * NV), pltpu.roll(proj1, NV, 1), grams)
+    grams = jnp.where(
+        jnp.logical_and(lane >= 2 * NV, lane < 3 * NV), pltpu.roll(proj, 2 * NV, 1), grams
+    )
+    gm[spot] = grams
 
     for device in mates:
         send(gm.at[spot], gm.at[spot], (g_send, g_recv), device)
@@ -327,6 +337,8 @@
     while len(sums) > 1:
         sums = [a + b for a, b in zip(sums[0::2], sums[1::2])]
     coef_ref[3] = sums[0] * (1.0 / PAIRS)
+    coef_ref[0] = pltpu.roll(gm[0], LANES - NV, 1)
+    coef_ref[2] = pltpu.roll(gm[0], LANES - 2 * NV, 1)
 
     for step in range(2):
         wait_bytes(cc.at[step, 0], cc_send.at[step])

time: 71.1 us -> 71 us (level)
  no operation moved by 1% of the time
where the time goes in v5:
time: 71 us; the launch traced here: 70.9 us
  Pallas kernels  70.3 us (99%)
    pallas_call x1, Pallas kernels, on_device(): pl.pallas_call(kernel, out_shape=(pltpu.VMEM((4,) + tile_shape, f32), plt...  68.8 us

profile of v5, /device:TPU:1, one launch (start us, length us, event | category | flops | bytes accessed | tf_op | source)
XLA Modules:
  0.0 70.9 jit_solution(14404794531743780029)
XLA Ops:
  0.6 68.8 %shard_map.59 = (f32[4,8,128]{2,1,0:T(8,128)S(1)}, f32[20,8,128]{2,1,0:T(8,128)S(1)}) custom-call(f32[20,8,128]{2,1,0:T(8,128)} %bitcast.5, bf16[2,20,256,128]{3,2,1,0:T(8,128)(2,1)} %bitcast.4, f32[20]{0:T(128)} %occ_hbm.1, f32[1,128]{1,0:T(1,128)} %bitcast.6), custom_call_target="tpu_custom_call" | custom-call | flops 200000000 | bytes 3000000 | tf_op jit(solution)/shard_map/pallas_call | solution.py:375
  69.5 1.4 %shard_map.60 = (f32[4,8,8]{2,1,0:T(8,128)}, f32[20,8,128]{2,1,0:T(8,128)}) custom-call(f32[4,8,128]{2,1,0:T(8,128)S(1)} %get-tuple-element.6.small_ref, f32[20,8,128]{2,1,0:T(8,128)S(1)} %get-tuple-element.7.resid_ref), custom_call_target="tpu_custom_call" | custom-call | flops 400000 | bytes 200000 | tf_op jit(solution)/shard_map/pallas_call | solution.py:414

commit v6 on v4

--- a/solution.py
+++ b/solution.py
@@ -155,7 +155,7 @@
     def wait_bytes(ref, sem):
         pltpu.make_async_copy(ref, ref, sem).wait()
 
-    def sum_group(step, tiles, first):
+    def sum_group(step, tiles, first, small_products):
         for index, value in enumerate(tiles):
             cc[step, core, index] = value
         if first:
@@ -164,6 +164,7 @@
             cc.at[step, core], cc.at[step, core], (cc_send.at[step], cc_recv.at[step]),
             {"vir": vir + 1 - 2 * core},
         )
+        hand_out(step, small_products())
         wait_bytes(cc.at[step, 0], cc_recv.at[step])
         for index in range(len(tiles)):
             cm[step, chip, index] = cc[step, 0, index] + cc[step, 1, index]
@@ -181,6 +182,18 @@
                 sums = [a + b for a, b in zip(sums[0::2], sums[1::2])]
             out.append(sums[0])
         return out
+
+    def hand_out(k, value):
+        gm[k, spot] = value
+        for device in mates:
+            send(gm.at[k, spot], gm.at[k, spot], (g_send.at[k], g_recv.at[k]), device)
+
+    def gather(k):
+        wait_bytes(gm.at[k, pl.ds(0, len(mates))], g_recv.at[k])
+        sums = [gm[k, j] for j in range(OCC_WAYS * VIR_WAYS)]
+        while len(sums) > 1:
+            sums = [a + b for a, b in zip(sums[0::2], sums[1::2])]
+        return sums[0]
 
     def send(source, target, sems, device):
         pltpu.make_async_remote_copy(
@@ -280,11 +293,12 @@
 
     vecs = [start[i] for i in range(ROWS)]
     shifted = [vecs[i] * delta(i) for i in range(ROWS)]
-    grams = columns(products(vecs, vecs) + products(vecs, shifted))
-    sums = contract(vecs, True)
-    *sums, grams = sum_group(0, sums + [grams], True)
+    sums = sum_group(
+        0, contract(vecs, True), True, lambda: columns(products(vecs, vecs) + products(vecs, shifted))
+    )
     part[0, ROWS] = columns(products([w * v for w, v in zip(weights, sums)], sums))
     back(0, sums)
+    grams = gather(0)
     lower = factor(grams * (1.0 / PAIRS))
     for index in range(4):
         xhat[index] = apply(lower, sums[index], NV)
@@ -300,12 +314,14 @@
     vecs = [r1[i] for i in range(ROWS)]
     moved = [delta(i) * q1[i] for i in range(ROWS)]
     shifted = [vecs[i] * delta(i) for i in range(ROWS)]
-    grams = columns(products(vecs, vecs) + products(vecs, shifted) + products(vecs, moved))
-    sums = contract(vecs, False)
-    *sums, grams = sum_group(1, sums + [grams], False)
+    sums = sum_group(
+        1, contract(vecs, False), False,
+        lambda: columns(products(vecs, vecs) + products(vecs, shifted) + products(vecs, moved)),
+    )
     scaled = [w * v for w, v in zip(weights, sums)]
     part[1, ROWS] = columns(products(scaled, sums) + products(scaled, [xhat[k] for k in range(4)]))
     back(1, sums)
+    grams = gather(1)
     lower = factor(grams * (1.0 / PAIRS))
     coef_ref[1] = jnp.where(lane >= row, lower, 0.0)
     for i in range(ROWS):
@@ -318,15 +334,8 @@
         resid_ref[i] = ag[1, i] + delta(i) * q2[i] - apply(proj, q2[i]) - apply(proj, q1[i], NV)
 
     vecs = [resid_ref[i] for i in range(ROWS)]
-    gm[spot] = columns(products(vecs, vecs))
-
-    for device in mates:
-        send(gm.at[spot], gm.at[spot], (g_send, g_recv), device)
-    wait_bytes(gm.at[pl.ds(0, OCC_WAYS * VIR_WAYS - 1)], g_recv)
-    sums = [gm[j] for j in range(OCC_WAYS * VIR_WAYS)]
-    while len(sums) > 1:
-        sums = [a + b for a, b in zip(sums[0::2], sums[1::2])]
-    coef_ref[3] = sums[0] * (1.0 / PAIRS)
+    hand_out(2, columns(products(vecs, vecs)))
+    coef_ref[3] = gather(2) * (1.0 / PAIRS)
 
     for step in range(2):
         wait_bytes(cc.at[step, 0], cc_send.at[step])
@@ -342,7 +351,8 @@
         def _():
             wait_bytes(part.at[step], rs_send.at[step])
 
-    wait_bytes(gm.at[pl.ds(0, OCC_WAYS * VIR_WAYS - 1)], g_send)
+    for k in range(3):
+        wait_bytes(gm.at[k, pl.ds(0, len(mates))], g_send.at[k])
 
 
 def finish(small_ref, resid_ref, coef_ref, next_ref):
@@ -377,17 +387,17 @@
             pltpu.VMEM((ROWS,) + tile_shape, f32),
             pltpu.VMEM((ROWS,) + tile_shape, f32),
             pltpu.VMEM((4,) + tile_shape, f32),
-            pltpu.VMEM((2, 2, 5) + tile_shape, f32),
-            pltpu.VMEM((2, CHIPS, 5) + tile_shape, f32),
+            pltpu.VMEM((2, 2, 4) + tile_shape, f32),
+            pltpu.VMEM((2, CHIPS, 4) + tile_shape, f32),
             pltpu.VMEM((2, TILES) + tile_shape, f32),
             pltpu.VMEM((2, NEAR, SHARE) + tile_shape, f32),
             pltpu.VMEM((2, BLOCKS, SHARE) + tile_shape, f32),
             pltpu.VMEM((2, TILES) + tile_shape, f32),
-            pltpu.VMEM((OCC_WAYS * VIR_WAYS,) + tile_shape, f32),
+            pltpu.VMEM((3, OCC_WAYS * VIR_WAYS) + tile_shape, f32),
             dma((3,)), dma((ROWS // GROUP,)),
             dma((2,)), dma((2,)), dma((2,)), dma((2,)),
             dma((2,)), dma((2,)), dma((2,)), dma((2,)), dma((2,)), dma((2,)),
-            dma, dma,
+            dma((3,)), dma((3,)),
         ],
         compiler_params=pltpu.CompilerParams(
             collective_id=0, has_side_effects=True, vmem_limit_bytes=60 * 1024 * 1024

time: 71.1 us -> 71 us (level)
  no operation moved by 1% of the time
where the time goes in v6:
time: 71 us; the launch traced here: 70.9 us
  Pallas kernels  70.2 us (99%)
    pallas_call x1, Pallas kernels, on_device(): pl.pallas_call(kernel, out_shape=(pltpu.VMEM((4,) + tile_shape, f32), plt...  68.8 us

profile of v6, /device:TPU:1, one launch (start us, length us, event | category | flops | bytes accessed | tf_op | source)
XLA Modules:
  0.0 70.9 jit_solution(17030560289530551480)
XLA Ops:
  0.6 68.8 %shard_map.59 = (f32[4,8,128]{2,1,0:T(8,128)S(1)}, f32[20,8,128]{2,1,0:T(8,128)S(1)}) custom-call(f32[20,8,128]{2,1,0:T(8,128)} %bitcast.5, bf16[2,20,256,128]{3,2,1,0:T(8,128)(2,1)} %bitcast.4, f32[20]{0:T(128)} %occ_hbm.1, f32[1,128]{1,0:T(1,128)} %bitcast.6), custom_call_target="tpu_custom_call" | custom-call | flops 200000000 | bytes 3000000 | tf_op jit(solution)/shard_map/pallas_call | solution.py:373
  69.5 1.4 %shard_map.60 = (f32[4,8,8]{2,1,0:T(8,128)}, f32[20,8,128]{2,1,0:T(8,128)}) custom-call(f32[4,8,128]{2,1,0:T(8,128)S(1)} %get-tuple-element.6.small_ref, f32[20,8,128]{2,1,0:T(8,128)S(1)} %get-tuple-element.7.resid_ref), custom_call_target="tpu_custom_call" | custom-call | flops 400000 | bytes 200000 | tf_op jit(solution)/shard_map/pallas_call | solution.py:412

commit v7 on v6

--- a/solution.py
+++ b/solution.py
@@ -201,18 +201,18 @@
             device_id=device, device_id_type=MESH,
         ).start()
 
-    def scatter(step):
+    def scatter(step, first, last):
         for d in range(1, NEAR):
             other = lax.rem(role + d, NEAR)
 
-            @pl.when(other < OWNERS)
+            @pl.when(jnp.logical_and(other >= first, other < last))
             def _():
                 send(
                     part.at[step, pl.ds(other * SHARE, SHARE)], rs.at[step, role],
                     (rs_send.at[step], rs_recv.at[step]), peers[d - 1],
                 )
 
-        @pl.when(owner)
+        @pl.when(jnp.logical_and(role >= first, role < last))
         def _():
             rs[step, role] = part[step, own]
 
@@ -232,7 +232,9 @@
             both = merge(both)
             part[step, i] = both[:, :LANES]
             part[step, i + 1] = both[:, LANES:]
-        scatter(step)
+            if i + 2 == 4 * SHARE:
+                scatter(step, 0, 4)
+        scatter(step, 4, OWNERS)
 
     def spread(step, lower, turned, extra):
         @pl.when(owner)

time: 71 us -> 71.3 us (level)
  no operation moved by 1% of the time
where the time goes in v7:
time: 71.3 us; the launch traced here: 71.1 us
  Pallas kernels  70.5 us (99%)
    pallas_call x1, Pallas kernels, on_device(): pl.pallas_call(kernel, out_shape=(pltpu.VMEM((4,) + tile_shape, f32), plt...  69.1 us

profile of v7, /device:TPU:1, one launch (start us, length us, event | category | flops | bytes accessed | tf_op | source)
XLA Modules:
  0.0 71.1 jit_solution(15081132898326110328)
XLA Ops:
  0.6 69.1 %shard_map.59 = (f32[4,8,128]{2,1,0:T(8,128)S(1)}, f32[20,8,128]{2,1,0:T(8,128)S(1)}) custom-call(f32[20,8,128]{2,1,0:T(8,128)} %bitcast.5, bf16[2,20,256,128]{3,2,1,0:T(8,128)(2,1)} %bitcast.4, f32[20]{0:T(128)} %occ_hbm.1, f32[1,128]{1,0:T(1,128)} %bitcast.6), custom_call_target="tpu_custom_call" | custom-call | flops 200000000 | bytes 3000000 | tf_op jit(solution)/shard_map/pallas_call | solution.py:375
  69.7 1.4 %shard_map.60 = (f32[4,8,8]{2,1,0:T(8,128)}, f32[20,8,128]{2,1,0:T(8,128)}) custom-call(f32[4,8,128]{2,1,0:T(8,128)S(1)} %get-tuple-element.6.small_ref, f32[20,8,128]{2,1,0:T(8,128)S(1)} %get-tuple-element.7.resid_ref), custom_call_target="tpu_custom_call" | custom-call | flops 400000 | bytes 200000 | tf_op jit(solution)/shard_map/pallas_call | solution.py:414
